TPU v7x, 512 devices: a whole 4x4x16 slice. The times are simulated.
512 devices in a mesh: dp: 32 (over z_lo, y, core), seq: 16 (over x, z_hi).
Axes of the slice: x: 4, y: 4, z: 16 (z_hi: 4, z_lo: 4; z = z_hi * 4 + z_lo), core: 2. Of those that a mesh axis runs over, the one named last changes fastest.
Arguments:
- out_gate: bfloat16 [32, 2048, 2048], P('dp', 'seq'), may hold values from -6 to 6
- in_gate: bfloat16 [32, 2048, 2048], P('dp', 'seq'), may hold values from -6 to 6
- signal: bfloat16 [32, 2048, 2048], P('dp', 'seq'), may hold values from -6 to 6
- upstream: bfloat16 [32, 2048, 2048], P('dp', 'seq'), may hold values from -6 to 6
- filter_taps: bfloat16 [2048, 2048], P('seq'), may hold values from -0.75 to 0.75
- skip_gain: float32 [2048], replicated, may hold values from -1 to 1
Outputs:
- grad_in_gate: bfloat16 [32, 2048, 2048], P('dp', 'seq')
- grad_signal: bfloat16 [32, 2048, 2048], P('dp', 'seq')
- grad_filter: float32 [2048, 2048], P('dp', 'seq')
All inputs are finite; a program needn't handle non-finite values.
Results may differ from a plain program's by a relative error of at most 0.008.
Values may be sent and summed in bfloat16 or wider, within the bound.
A program may use at most 128 MiB of HBM per device.

v0:
```python
import math

import jax
import jax.numpy as jnp
from jax import lax
from jax.sharding import PartitionSpec as P

highest = lax.Precision.HIGHEST


def angle_table(rows, cols, period):
    product = lax.iota(jnp.int32, rows)[:, None] * lax.iota(jnp.int32, cols)[None, :] % period
    phase = product.astype(jnp.float32) * (2.0 * math.pi / period)
    return (jnp.cos(phase), jnp.sin(phase))


def pick_factor(full_span):
    for candidate in range(2, full_span + 1, 2):
        if full_span % candidate == 0 and candidate * candidate >= full_span:
            return candidate
    return full_span


def forward_dft(real_series, imag_series, first, second):
    half = first // 2
    channels = real_series.shape[1]
    outer_cosine, outer_sine = angle_table(first, half, first)
    table = jnp.concatenate([outer_cosine, outer_sine], 0)
    upper = table.astype(jnp.bfloat16)
    lower = (table - upper.astype(jnp.float32)).astype(jnp.bfloat16)
    stacked_table = jnp.concatenate([upper, lower], 0)
    if imag_series is None:
        data = real_series.reshape(1, half, second, channels)
    else:
        data = jnp.stack(
            [
                real_series.reshape(half, second, channels),
                imag_series.reshape(half, second, channels),
            ],
            0,
        )
    product = jnp.einsum("ka,parc->pkrc", stacked_table, data, preferred_element_type=jnp.float32)
    both = product[:, : 2 * first] + product[:, 2 * first :]
    cosine_part = both[:, :first]
    sine_part = both[:, first:]
    if imag_series is None:
        real_one = cosine_part[0]
        imag_one = -sine_part[0]
    else:
        real_one = cosine_part[0] + sine_part[1]
        imag_one = cosine_part[1] - sine_part[0]
    twist_cosine, twist_sine = angle_table(first, second, first * second)
    twist_cosine = twist_cosine[:, :, None]
    twist_sine = twist_sine[:, :, None]
    real_two = real_one * twist_cosine + imag_one * twist_sine
    imag_two = imag_one * twist_cosine - real_one * twist_sine
    inner_cosine, inner_sine = angle_table(second, second, second)
    inner_table = jnp.stack(
        [jnp.stack([inner_cosine, -inner_sine], 1), jnp.stack([inner_sine, inner_cosine], 1)], 0
    )
    spectrum = jnp.einsum(
        "pkrc,prqm->qkmc", jnp.stack([real_two, imag_two], 0), inner_table, precision=highest
    )
    return (spectrum[0], spectrum[1])


def inverse_dft(real_in, imag_in, first, second):
    half = first // 2
    channels = real_in.shape[2]
    inner_cosine, inner_sine = angle_table(second, second, second)
    inner_table = jnp.stack(
        [jnp.stack([inner_cosine, inner_sine], 1), jnp.stack([-inner_sine, inner_cosine], 1)], 0
    )
    section_one = jnp.einsum(
        "pkmc,pmqr->qkrc", jnp.stack([real_in, imag_in], 0), inner_table, precision=highest
    )
    real_one = section_one[0]
    imag_one = section_one[1]
    twist_cosine, twist_sine = angle_table(first, second, first * second)
    twist_cosine = twist_cosine[:, :, None]
    twist_sine = twist_sine[:, :, None]
    real_two = real_one * twist_cosine - imag_one * twist_sine
    imag_two = real_one * twist_sine + imag_one * twist_cosine
    outer_cosine, outer_sine = angle_table(half, first, first)
    outer_table = jnp.stack(
        [jnp.stack([outer_cosine, -outer_sine], 0), jnp.stack([outer_sine, outer_cosine], 0)], 0
    )
    series = jnp.einsum(
        "qpak,pkrc->qarc", outer_table, jnp.stack([real_two, imag_two], 0), precision=highest
    )
    return series.reshape(2, half * second, channels) * (1.0 / (first * second))


def on_device(out_gate, in_gate, signal, upstream, filter_taps, skip_gain):
    gated_grad = (upstream[0].astype(jnp.float32) * out_gate[0].astype(jnp.float32)).astype(
        jnp.bfloat16
    )
    conv_input = (in_gate[0].astype(jnp.float32) * signal[0].astype(jnp.float32)).astype(
        jnp.bfloat16
    )
    grad_cols, input_cols, filter_cols = (
        lax.all_to_all(gated_grad, "seq", split_axis=1, concat_axis=0, tiled=True),
        lax.all_to_all(conv_input, "seq", split_axis=1, concat_axis=0, tiled=True),
        lax.all_to_all(filter_taps, "seq", split_axis=1, concat_axis=0, tiled=True),
    )
    full_span = 2 * grad_cols.shape[0]
    first = pick_factor(full_span)
    second = full_span // first
    grad_real, grad_imag = forward_dft(grad_cols, None, first, second)
    mixed_real, mixed_imag = forward_dft(filter_cols, -input_cols, first, second)
    combined = inverse_dft(
        grad_real * mixed_real + grad_imag * mixed_imag,
        grad_imag * mixed_real - grad_real * mixed_imag,
        first,
        second,
    )
    back_conv = combined[0].astype(jnp.bfloat16)
    lag_terms = combined[1]
    returned = lax.all_to_all(back_conv, "seq", split_axis=0, concat_axis=1, tiled=True)
    lag_share = lax.psum_scatter(lag_terms, "dp", scatter_dimension=0, tiled=True) * (
        1.0 / lax.axis_size("dp")
    )
    input_grad = returned.astype(jnp.float32) + skip_gain[None, :] * gated_grad.astype(jnp.float32)
    grad_in_gate = (input_grad * signal[0].astype(jnp.float32)).astype(jnp.bfloat16)[None]
    grad_signal = (input_grad * in_gate[0].astype(jnp.float32)).astype(jnp.bfloat16)[None]
    return (grad_in_gate, grad_signal, lag_share)


def solution(mesh):
    return jax.shard_map(
        on_device,
        mesh=mesh,
        in_specs=(
            P("dp", "seq", None),
            P("dp", "seq", None),
            P("dp", "seq", None),
            P("dp", "seq", None),
            P("seq", None),
            P(),
        ),
        out_specs=(P("dp", "seq", None), P("dp", "seq", None), P("dp", "seq")),
        check_vma=False,
    )
```

profile of v0, /device:TPU:1, one launch (start us, length us, event | category | flops | bytes accessed | tf_op | source)
XLA Modules:
  0.0 382.1 jit_solution(12137733148204186591)
XLA Ops:
  10.8 18.2 %all-to-all-start.2 = ((bf16[128,16,128]{0,2,1:T(8,128)(2,1)}), bf16[128,16,128]{0,2,1:T(8,128)(2,1)S(1)}, u32[]{:S(2)}, u32[]{:S(2)}) async-start(bf16[128,16,128]{0,2,1:T(8,128)(2,1)} %bitcast.27), calls=%async_computation.2 | async-start | bytes 1048576 | tf_op jit(solution)/shard_map/all_to_all | solution.py:103
  30.1 26.2 %all-to-all-done.2 = bf16[128,16,128]{0,2,1:T(8,128)(2,1)S(1)} async-done(((bf16[128,16,128]{0,2,1:T(8,128)(2,1)}), bf16[128,16,128]{0,2,1:T(8,128)(2,1)S(1)}, u32[]{:S(2)}, u32[]{:S(2)}) %all-to-all-start.2) | async-done | bytes 524320 | tf_op jit(solution)/shard_map/all_to_all | solution.py:103
  56.2 8.5 %all-to-all-start.1 = ((bf16[128,16,128]{0,2,1:T(8,128)(2,1)}), bf16[128,16,128]{0,2,1:T(8,128)(2,1)S(1)}, u32[]{:S(2)}, u32[]{:S(2)}) async-start(bf16[128,16,128]{0,2,1:T(8,128)(2,1)} %bitcast.24), calls=%async_computation.1 | async-start | bytes 1048576 | tf_op jit(solution)/shard_map/all_to_all | solution.py:104
  68.4 16.8 %all-to-all-done.1 = bf16[128,16,128]{0,2,1:T(8,128)(2,1)S(1)} async-done(((bf16[128,16,128]{0,2,1:T(8,128)(2,1)}), bf16[128,16,128]{0,2,1:T(8,128)(2,1)S(1)}, u32[]{:S(2)}, u32[]{:S(2)}) %all-to-all-start.1) | async-done | bytes 524320 | tf_op jit(solution)/shard_map/all_to_all | solution.py:104
  85.2 4.4 %all-to-all-start = ((bf16[128,16,128]{0,2,1:T(8,128)(2,1)}), bf16[128,16,128]{0,2,1:T(8,128)(2,1)}, u32[]{:S(2)}, u32[]{:S(2)}) async-start(bf16[128,16,128]{0,2,1:T(8,128)(2,1)} %bitcast.12), calls=%async_computation | async-start | bytes 1048576 | tf_op jit(solution)/shard_map/all_to_all | solution.py:102
  92.2 8.1 %convolution_bitcast_fusion = f32[2,256,64,128]{1,3,2,0:T(8,128)} fusion(bf16[1,32,64,128]{3,1,2,0:T(8,128)(2,1)S(1)} %copy.40, bf16[1,32,64,128]{3,1,2,0:T(8,128)(2,1)S(1)} %copy.39, bf16[128,32]{0,1:T(8,128)(2,1)S(1)} %subtract_convert_fusion, bf16[128,32]{0,1:T(8,128)(2,1)S(1)} %fusion.71), kind=kOutput, calls=%fused_computation.7 | convolution fusion | flops 268992512 | bytes 17842176 | tf_op jit(solution)/shard_map/ka,parc->pkrc/dot_general | solution.py:42
  100.3 11.7 %slice_add_fusion = f32[2,128,64,128]{1,3,2,0:T(8,128)} fusion(f32[2,256,64,128]{1,3,2,0:T(8,128)} %convolution_bitcast_fusion), kind=kLoop, calls=%fused_computation | loop fusion | flops 2097152 | bytes 25165824 | tf_op jit(solution)/shard_map/add | solution.py:43
  115.6 1.5 slice-done.1
  117.1 7.4 %multiply_add_fusion.2 = (f32[1,64,64,128]{1,3,2,0:T(8,128)}, f32[1,64,64,128]{1,3,2,0:T(8,128)}, f32[1,64,64,128]{1,3,2,0:T(8,128)}, f32[1,64,64,128]{1,3,2,0:T(8,128)}) fusion(f32[1,128,64,128]{1,3,2,0:T(8,128)S(1)} %slice_add_fusion.2, f32[64,64]{0,1:T(8,128)S(1)} %get-tuple-element.28, f32[64,64]{0,1:T(8,128)S(1)} %get-tuple-element.29, ...), kind=kLoop, calls=%fused_computation.25 | loop fusion | flops 7864320 | bytes 21004288 | tf_op jit(solution)/shard_map/add | solution.py:55
  124.5 8.4 %pad_maximum_fusion = f32[2,64,64,128]{1,3,2,0:T(8,128)} fusion(f32[1,64,64,128]{1,3,2,0:T(8,128)} %get-tuple-element.13, f32[1,64,64,128]{1,3,2,0:T(8,128)} %get-tuple-element.12), kind=kLoop, calls=%fused_computation.1 | loop fusion | flops 1048576 | bytes 8388608 | tf_op jit(solution)/shard_map/stack | solution.py:62
  132.8 7.3 %copy.33 = f32[2,64,64,128]{3,2,0,1:T(8,128)} copy(f32[2,64,64,128]{1,3,2,0:T(8,128)} %pad_maximum_fusion) | data formatting | bytes 8388608 | tf_op jit(solution)/shard_map/stack | solution.py:62
  140.2 8.4 %pad_maximum_fusion.1 = f32[2,64,64,128]{1,3,2,0:T(8,128)} fusion(f32[1,64,64,128]{1,3,2,0:T(8,128)} %get-tuple-element.20, f32[1,64,64,128]{1,3,2,0:T(8,128)} %get-tuple-element.21), kind=kLoop, calls=%fused_computation.2 | loop fusion | flops 1048576 | bytes 8388608 | tf_op jit(solution)/shard_map/stack | solution.py:62
  148.5 7.3 %copy.41 = f32[2,64,64,128]{3,2,0,1:T(8,128)} copy(f32[2,64,64,128]{1,3,2,0:T(8,128)} %pad_maximum_fusion.1) | data formatting | bytes 8388608 | tf_op jit(solution)/shard_map/stack | solution.py:62
  155.9 5.7 %fusion.10 = f32[2,64,64,128]{3,2,1,0:T(8,128)S(1)} fusion(f32[2,64,64,128]{3,2,0,1:T(8,128)} %copy.33, f32[1,64,2,64]{1,3,0,2:T(8,128)S(1)} %get-tuple-element.17, f32[1,64,2,64]{1,3,0,2:T(8,128)S(1)} %get-tuple-element.22), kind=kOutput, calls=%fused_computation.27 | convolution fusion | flops 1610629120 | bytes 8454144 | tf_op jit(solution)/shard_map/pkrc,prqm->qkmc/dot_general | solution.py:61
  161.5 4.1 %fusion.13 = f32[2,64,64,128]{3,2,1,0:T(8,128)S(1)} fusion(f32[2,64,64,128]{3,2,0,1:T(8,128)S(1)} %copy-done, f32[1,64,2,64]{1,3,0,2:T(8,128)S(1)} %get-tuple-element.17, f32[1,64,2,64]{1,3,0,2:T(8,128)S(1)} %get-tuple-element.22), kind=kOutput, calls=%fused_computation.28 | convolution fusion | flops 1610629120 | bytes 8454144 | tf_op jit(solution)/shard_map/pkrc,prqm->qkmc/dot_general | solution.py:61
  167.1 5.6 %fusion.16 = f32[2,64,64,128]{3,1,2,0:T(8,128)} fusion(f32[1,64,64,128]{3,2,1,0:T(8,128)S(1)} %get-tuple-element.11, f32[1,64,64,128]{3,2,1,0:T(8,128)S(1)} %get-tuple-element.10, f32[1,64,2,64]{1,3,2,0:T(8,128)S(1)} %get-tuple-element.23, f32[1,64,2,64]{1,3,2,0:T(8,128)S(1)} %get-tuple-element.16), kind=kOutput, calls=%fused_computation.29 | convolution fusion | flops 1611677696 | bytes 8454144 | tf_op jit(solution)/shard_map/pkmc,pmqr->qkrc/dot_general | solution.py:74
  172.7 7.0 %copy.44 = f32[2,64,64,128]{2,3,1,0:T(8,128)} copy(f32[2,64,64,128]{3,1,2,0:T(8,128)} %fusion.16) | data formatting | bytes 8388608 | tf_op jit(solution)/shard_map/pkmc,pmqr->qkrc/dot_general | solution.py:74
  179.7 4.7 %multiply_subtract_fusion = (f32[1,64,64,128]{1,3,2,0:T(8,128)S(1)}, f32[1,64,64,128]{1,3,2,0:T(8,128)S(1)}) fusion(f32[2,64,64,128]{1,3,2,0:T(8,128)} %bitcast.106, f32[64,64]{0,1:T(8,128)S(1)} %get-tuple-element.28, f32[64,64]{0,1:T(8,128)S(1)} %get-tuple-element.29), kind=kLoop, calls=%fused_computation.21 | loop fusion | flops 3145728 | bytes 8421376 | tf_op jit(solution)/shard_map/sub | solution.py:82
  184.5 7.9 %bitcast_multiply_fusion = f32[2,32,64,128]{3,1,2,0:T(8,128)S(1)} fusion(f32[1,64,64,128]{1,3,2,0:T(8,128)S(1)} %get-tuple-element.7, f32[1,64,64,128]{1,3,2,0:T(8,128)S(1)} %get-tuple-element.6, f32[1,2,32,64]{3,2,1,0:T(8,128)S(1)} %get-tuple-element.25, f32[1,2,32,64]{3,2,1,0:T(8,128)S(1)} %get-tuple-element.24), kind=kOutput, calls=%fused_computation.30 | convolution fusion | flops 806887424 | bytes 6324224 | tf_op jit(solution)/shard_map/qpak,pkrc->qarc/dot_general | solution.py:88
  193.5 13.6 %all-to-all-start.3 = ((bf16[16,128,128]{2,1,0:T(8,128)(2,1)}), bf16[16,128,128]{2,1,0:T(8,128)(2,1)}, u32[]{:S(2)}, u32[]{:S(2)}) async-start(bf16[16,128,128]{2,1,0:T(8,128)(2,1)} %bitcast.110), calls=%async_computation.3 | async-start | bytes 1048576 | tf_op jit(solution)/shard_map/all_to_all | solution.py:119
  207.2 1.6 copy.48
  208.9 15.5 %all-to-all-done.3 = bf16[16,128,128]{2,1,0:T(8,128)(2,1)} async-done(((bf16[16,128,128]{2,1,0:T(8,128)(2,1)}), bf16[16,128,128]{2,1,0:T(8,128)(2,1)}, u32[]{:S(2)}, u32[]{:S(2)}) %all-to-all-start.3) | async-done | bytes 524320 | tf_op jit(solution)/shard_map/all_to_all | solution.py:119
  225.9 1.5 fusion.19
  229.4 144.4 %reduce-scatter.2.cloned.1.call-done = f32[64,128]{1,0:T(8,128)} async-done(((f32[2048,128]{1,0:T(8,128)}), f32[64,128]{1,0:T(8,128)}) %reduce-scatter.2.cloned.1.call-update) | async-done | bytes 32784 | tf_op jit(solution)/shard_map/reduce_scatter | solution.py:120
  (49 shorter events, 21.8 us)
Async XLA Ops:
  7.2 21.9 %copy-start.1 = (bf16[128,2048]{1,0:T(8,128)(2,1)S(1)}, bf16[128,2048]{1,0:T(8,128)(2,1)}, u32[]{:S(2)}) copy-start(bf16[128,2048]{1,0:T(8,128)(2,1)} %param.10) | copy-start | bytes 1572868
  7.2 57.6 %copy-start.2 = (bf16[1,128,2048]{2,1,0:T(8,128)(2,1)S(1)}, bf16[1,128,2048]{2,1,0:T(8,128)(2,1)}, u32[]{:S(2)}) copy-start(bf16[1,128,2048]{2,1,0:T(8,128)(2,1)} %param.9) | copy-start | bytes 1572868
  10.8 45.4 %all-to-all-start.2 = ((bf16[128,16,128]{0,2,1:T(8,128)(2,1)}), bf16[128,16,128]{0,2,1:T(8,128)(2,1)S(1)}, u32[]{:S(2)}, u32[]{:S(2)}) async-start(bf16[128,16,128]{0,2,1:T(8,128)(2,1)} %bitcast.27), calls=%async_computation.2 | async-start | bytes 1048576 | tf_op jit(solution)/shard_map/all_to_all | solution.py:103
  56.2 28.9 %all-to-all-start.1 = ((bf16[128,16,128]{0,2,1:T(8,128)(2,1)}), bf16[128,16,128]{0,2,1:T(8,128)(2,1)S(1)}, u32[]{:S(2)}, u32[]{:S(2)}) async-start(bf16[128,16,128]{0,2,1:T(8,128)(2,1)} %bitcast.24), calls=%async_computation.1 | async-start | bytes 1048576 | tf_op jit(solution)/shard_map/all_to_all | solution.py:104
  85.2 26.9 %all-to-all-start = ((bf16[128,16,128]{0,2,1:T(8,128)(2,1)}), bf16[128,16,128]{0,2,1:T(8,128)(2,1)}, u32[]{:S(2)}, u32[]{:S(2)}) async-start(bf16[128,16,128]{0,2,1:T(8,128)(2,1)} %bitcast.12), calls=%async_computation | async-start | bytes 1048576 | tf_op jit(solution)/shard_map/all_to_all | solution.py:102
  113.4 2.2 slice-start
  114.7 2.4 slice-start.1
  155.9 5.7 %copy-start = (f32[2,64,64,128]{3,2,0,1:T(8,128)S(1)}, f32[2,64,64,128]{3,2,0,1:T(8,128)}, u32[]{:S(2)}) copy-start(f32[2,64,64,128]{3,2,0,1:T(8,128)} %copy.41) | copy-start | bytes 12582916
  193.5 30.9 %all-to-all-start.3 = ((bf16[16,128,128]{2,1,0:T(8,128)(2,1)}), bf16[16,128,128]{2,1,0:T(8,128)(2,1)}, u32[]{:S(2)}, u32[]{:S(2)}) async-start(bf16[16,128,128]{2,1,0:T(8,128)(2,1)} %bitcast.110), calls=%async_computation.3 | async-start | bytes 1048576 | tf_op jit(solution)/shard_map/all_to_all | solution.py:119
  207.1 18.7 %copy-start.3 = (f32[2048]{0:T(1024)S(1)}, f32[2048]{0:T(1024)}, u32[]{:S(2)}) copy-start(f32[2048]{0:T(1024)} %param.11) | copy-start | bytes 24580
  207.1 166.7 %reduce-scatter.2.cloned.1.call-start = ((), (), s32[]{:S(2)}) async-start(), calls=%async_computation.5 | async-start | bytes 1081344 | tf_op jit(solution)/shard_map/reduce_scatter | solution.py:120
Sparse Core Ops, SparseCore 0:
  210.7 163.0 reduce-scatter.1
where the time goes:
time: 387 us; the launch traced here: 382 us
  waiting for transfers between devices  203 us (52%)
  other arithmetic  50.9 us (13%)
  starting transfers between devices  44.8 us (12%)
  local copies, waits for them, and re-layouts  36.5 us (9%)
  matrix products  32.7 us (8%)
  between operations  14.3 us (4%)
    reduce_scatter x1, waiting for transfers between devices, on_device(): lax.psum_scatter(lag_terms, 'dp', scatter_dimension=0, tiled=True)  144 us
    all_to_all x1, waiting for transfers between devices, on_device(): lax.all_to_all(conv_input, 'seq', split_axis=1, concat_axis=0, tiled=True)  26.2 us
    all_to_all x1, starting transfers between devices, on_device(): lax.all_to_all(conv_input, 'seq', split_axis=1, concat_axis=0, tiled=True)  18.2 us
    all_to_all x1, waiting for transfers between devices, on_device(): lax.all_to_all(filter_taps, 'seq', split_axis=1, concat_axis=0, tiled=True)  16.8 us
    another operation x2, other arithmetic, forward_dft(): jnp.stack([real_two, imag_two], 0)  16.7 us
    all_to_all x1, waiting for transfers between devices, on_device(): lax.all_to_all(back_conv, 'seq', split_axis=0, concat_axis=1, tiled=True)  15.5 us
    another operation x2, local copies, waits for them, and re-layouts, forward_dft(): jnp.stack([real_two, imag_two], 0)  14.7 us
    all_to_all x1, starting transfers between devices, on_device(): lax.all_to_all(back_conv, 'seq', split_axis=0, concat_axis=1, tiled=True)  13.6 us
  transfers between devices with their start and end apart: 5, of which 4 were waited for; matrix products, arithmetic and copies ran while one was open for 9% of the time, Pallas kernels for 0%

commit v1 on v0

v1 whole, which is shorter than its diff:
```python
import jax
import jax.numpy as jnp
from jax import lax
from jax.experimental import pallas as pl
from jax.experimental.pallas import tpu as pltpu
from jax.sharding import PartitionSpec as P

MESH = pl.DeviceIdType.MESH
f32 = jnp.float32
bf16 = jnp.bfloat16

Z_ORDER = (2, 1, 3, 0)
SEQ_OFFS = [(dx, dz) for dz in Z_ORDER for dx in range(4) if (dx, dz) != (0, 0)]
SEQ_SLOT = {off: i for i, off in enumerate(SEQ_OFFS)}


def kernel(
    og, ig, sg, up, ft, skip,
    oa, ob, of,
    gT, uT, hT, g1, u1, H, G, U, BC, R1, bT, Gf, Uf, Bf, HR, Lp, L, LZ, LS, LQ,
    g1s, g1r, u1s, u1r, hs, hr, g2s, g2r, u2s, u2r, b2s, b2r, b1s, b1r, lzs, lzr, lqs, lqr,
):
    dp = lax.axis_index("dp")
    sq = lax.axis_index("seq")
    x, zh = sq // 4, sq % 4
    zl, q = dp // 8, dp % 8

    def seq_index(dx, dz, sign):
        return ((x + sign * dx + 4) % 4) * 4 + (zh + sign * dz + 4) % 4

    def seq_dev(dx, dz, sign=1):
        return (dp, seq_index(dx, dz, sign))

    def q_index(k, sign=1):
        return (q + sign * k + 8) % 8

    def q_dev(k, sign=1):
        return (zl * 8 + q_index(k, sign), sq)

    def zl_index(k, sign=1):
        return (zl + sign * k + 4) % 4

    def zl_dev(k, sign=1):
        return (zl_index(k, sign) * 8 + q, sq)

    def remote(src, dst, ssem, rsem, dev):
        return pltpu.make_async_remote_copy(
            src_ref=src, dst_ref=dst, send_sem=ssem, recv_sem=rsem,
            device_id=dev, device_id_type=MESH,
        )

    barrier = pltpu.get_barrier_semaphore()
    for dx, dz in SEQ_OFFS:
        pl.semaphore_signal(barrier, inc=1, device_id=seq_dev(dx, dz), device_id_type=MESH)
    for k in range(1, 8):
        pl.semaphore_signal(barrier, inc=1, device_id=q_dev(k), device_id_type=MESH)
    for k in range(1, 4):
        pl.semaphore_signal(barrier, inc=1, device_id=zl_dev(k), device_id_type=MESH)

    def gated(a_ref, b_ref, cols):
        return (a_ref[:, cols].astype(f32) * b_ref[:, cols].astype(f32)).astype(bf16)

    def prepare(a_ref, b_ref, out):
        def body(k, carry):
            cols = pl.ds(pl.multiple_of(k * 128, 128), 128)
            out[k] = gated(a_ref, b_ref, cols).astype(f32).T.astype(bf16)
            return carry
        lax.fori_loop(0, 16, body, 0)

    prepare(up, og, gT)

    pl.semaphore_wait(barrier, 25)

    def scatter(send, recv, ss, rs):
        copies = {}
        for i, (dx, dz) in enumerate(SEQ_OFFS):
            t = seq_index(dx, dz, 1)
            c = remote(send.at[t], recv.at[x, zh], ss.at[i], rs.at[i], seq_dev(dx, dz))
            c.start()
            copies[(dx, dz)] = c
        return copies

    cg = scatter(gT, g1, g1s, g1r)

    def hbody(k, carry):
        cols = pl.ds(pl.multiple_of(k * 128, 128), 128)
        hT[k] = ft[:, cols].astype(f32).T.astype(bf16)
        return carry
    lax.fori_loop(0, 16, hbody, 0)
    mine = pl.ds(pl.multiple_of(q * 16, 16), 16)
    ch = []
    for i, (dx, dz) in enumerate(SEQ_OFFS):
        t = seq_index(dx, dz, 1)
        c = remote(hT.at[t, mine], H.at[sq], hs.at[i], hr.at[i], seq_dev(dx, dz))
        c.start()
        ch.append(c)
    H[sq] = hT[sq, mine, :]

    prepare(ig, sg, uT)
    cu = scatter(uT, u1, u1s, u1r)
    g1[x, zh] = gT[sq]
    u1[x, zh] = uT[sq]

    def spread(first, cs, stage, out, ss, rs):
        copies = []
        for n, dz in enumerate(Z_ORDER):
            for dx in range(4):
                if (dx, dz) != (0, 0):
                    cs[(dx, dz)].wait_recv()
            zsrc = (zh - dz + 4) % 4
            for k in range(1, 8):
                t = pl.ds(pl.multiple_of(q_index(k) * 16, 16), 16)
                c = remote(
                    first.at[:, zsrc, t, :], out.at[:, zsrc, q],
                    ss.at[n, k - 1], rs.at[n, k - 1], q_dev(k),
                )
                c.start()
                copies.append(c)
            out[:, zsrc, q] = first[:, zsrc, mine, :]
        return copies

    cg2 = spread(g1, cg, 0, G, g2s, g2r)

    row = lax.broadcasted_iota(jnp.int32, (128, 128), 0)
    col = lax.broadcasted_iota(jnp.int32, (128, 128), 1)
    lower = col <= row
    flip = jnp.where(row + col == 127, 1.0, 0.0).astype(bf16)

    for c in ch:
        c.wait_recv()
    HR[...] = jnp.dot(H[...].reshape(256, 128), flip, preferred_element_type=f32)

    for c in cg2:
        c.wait_recv()
    Gf[...] = G[...].reshape(2048, 128).astype(f32)

    def shifted(c):
        rows = Gf[pl.ds(c, 128, stride=16), :]
        zero = jnp.zeros((128, 128), f32)
        even = jnp.concatenate([rows, zero], 0).astype(bf16)
        odd = jnp.concatenate([rows[8:], zero, zero[:8]], 0).astype(bf16)
        return [(even, odd)[d % 2][(d // 2) * 16:(d // 2) * 16 + 128] for d in range(16)]

    def conv_body(c, carry):
        gs = shifted(c)
        h = HR[pl.ds(c, 16, stride=16), :]
        prev = jnp.zeros((128, 128), f32)
        total = jnp.zeros((128, 128), f32)
        for e in range(8):
            ws = []
            for d in (2 * e, 2 * e + 1):
                rolled = pltpu.roll(
                    jnp.broadcast_to(h[d:d + 1], (128, 128)), 1, 1, stride=1, stride_axis=0
                )
                ws.append(jnp.where(lower, rolled, prev).astype(bf16))
                prev = rolled
            total += jnp.dot(
                jnp.concatenate([gs[2 * e], gs[2 * e + 1]], 1), jnp.concatenate(ws, 0),
                preferred_element_type=f32,
            )
        Bf[pl.ds(c, 128, stride=16), :] = total
        return carry
    lax.fori_loop(0, 16, conv_body, 0)
    BC[...] = Bf[...].astype(bf16).reshape(4, 4, 8, 16, 128)

    cb2 = []
    for n, dz in enumerate(Z_ORDER):
        zt = (zh + dz) % 4
        group = []
        for k in range(1, 8):
            c = remote(
                BC.at[:, zt, q_index(k)], R1.at[:, zt, mine, :],
                b2s.at[n, k - 1], b2r.at[n, k - 1], q_dev(k),
            )
            c.start()
            group.append(c)
        R1[:, zt, mine, :] = BC[:, zt, q]
        cb2.append(group)
    cb1 = {}
    for n, dz in enumerate(Z_ORDER):
        for c in cb2[n]:
            c.wait_recv()
        zt = (zh + dz) % 4
        for dx in range(4):
            if (dx, dz) == (0, 0):
                continue
            i = SEQ_SLOT[(dx, dz)]
            c = remote(
                R1.at[(x + dx) % 4, zt], bT.at[sq], b1s.at[i], b1r.at[i], seq_dev(dx, dz)
            )
            c.start()
            cb1[(dx, dz)] = c
    bT[sq] = R1[x, zh]

    cu2 = spread(u1, cu, 1, U, u2s, u2r)
    for c in cu2:
        c.wait_recv()
    Uf[...] = jnp.dot(U[...].reshape(2048, 128), flip, preferred_element_type=f32)

    def lag_body(c, carry):
        gs = shifted(c)
        ut = Uf[pl.ds(c, 128, stride=16), :].T.astype(bf16)
        prev = None
        for e in range(8):
            m = jnp.dot(
                ut, jnp.concatenate([gs[2 * e], gs[2 * e + 1]], 1), preferred_element_type=f32
            )
            for d in (2 * e, 2 * e + 1):
                part = m[:, (d % 2) * 128:(d % 2) * 128 + 128]
                rolled = pltpu.roll(part, 1, 1, stride=1, stride_axis=0)
                if prev is not None:
                    Lp[pl.ds(pl.multiple_of(((d - 1) * 16 + c) * 8, 8), 8), :] = jnp.sum(
                        jnp.where(lower, prev, rolled).reshape(16, 8, 128), 0
                    )
                prev = rolled
        Lp[pl.ds(pl.multiple_of((15 * 16 + c) * 8, 8), 8), :] = jnp.sum(
            jnp.where(lower, prev, 0.0).reshape(16, 8, 128), 0
        )
        return carry
    lax.fori_loop(0, 16, lag_body, 0)

    lags = Lp[pl.ds(0, 256, stride=8), :]
    for k in range(1, 8):
        lags += Lp[pl.ds(k, 256, stride=8), :]
    L[...] = lags.reshape(16, 16, 128)

    clz = []
    for k in range(1, 4):
        c = remote(
            L.at[pl.ds(zl_index(k) * 4, 4)], LZ.at[k - 1],
            lzs.at[k - 1], lzr.at[k - 1], zl_dev(k),
        )
        c.start()
        clz.append(c)
    for c in clz:
        c.wait_recv()
    LS[...] = L[pl.ds(zl * 4, 4)] + LZ[0] + LZ[1] + LZ[2]
    clq = []
    for k in range(1, 8):
        c = remote(
            LS.at[q_index(k) // 2], LQ.at[q], lqs.at[k - 1], lqr.at[k - 1], q_dev(k)
        )
        c.start()
        clq.append(c)
    LQ[q] = LS[q // 2]
    for c in clq:
        c.wait_recv()
    table = LQ[...].reshape(128, 128).T
    of[...] = jnp.where(q % 2 == 0, table[:64], table[64:]) * (1.0 / 32.0)

    def finish(blk):
        cols = pl.ds(pl.multiple_of(blk * 128, 128), 128)
        back = bT[blk].astype(f32).T
        total = back + skip[:, cols] * gated(up, og, cols).astype(f32)
        oa[:, cols] = (total * sg[:, cols].astype(f32)).astype(bf16)
        ob[:, cols] = (total * ig[:, cols].astype(f32)).astype(bf16)

    for off in SEQ_OFFS:
        cb1[off].wait_recv()

    def ebody(k, carry):
        finish(k)
        return carry
    lax.fori_loop(0, 16, ebody, 0)

    for c in (
        list(cg.values()) + list(cu.values()) + ch + cg2 + cu2
        + [c for g in cb2 for c in g] + list(cb1.values()) + clz + clq
    ):
        c.wait_send()


def on_device(out_gate, in_gate, signal, upstream, filter_taps, skip_gain):
    vm = lambda shape, dtype: pltpu.VMEM(shape, dtype)
    dma = pltpu.SemaphoreType.DMA
    blocks = (16, 128, 128)
    quad = (4, 4, 128, 128)
    owned = (4, 4, 8, 16, 128)
    scratch = [
        vm(blocks, bf16), vm(blocks, bf16), vm(blocks, bf16),
        vm(quad, bf16), vm(quad, bf16),
        vm((16, 16, 128), bf16),
        vm(owned, bf16), vm(owned, bf16), vm(owned, bf16),
        vm(quad, bf16), vm(blocks, bf16),
        vm((2048, 128), f32), vm((2048, 128), f32), vm((2048, 128), f32),
        vm((256, 128), f32), vm((2048, 128), f32),
        vm((16, 16, 128), f32), vm((3, 4, 16, 128), f32),
        vm((4, 16, 128), f32), vm((8, 16, 128), f32),
    ]
    for shape in ((15,), (15,), (15,), (4, 7), (4, 7), (4, 7), (15,), (3,), (7,)):
        scratch += [dma(shape), dma(shape)]
    spec = pl.BlockSpec(memory_space=pltpu.VMEM)
    a, b, lag = pl.pallas_call(
        kernel,
        out_shape=(
            jax.ShapeDtypeStruct((128, 2048), bf16),
            jax.ShapeDtypeStruct((128, 2048), bf16),
            jax.ShapeDtypeStruct((64, 128), f32),
        ),
        in_specs=[spec] * 6,
        out_specs=(spec,) * 3,
        scratch_shapes=scratch,
        compiler_params=pltpu.CompilerParams(
            collective_id=0, has_side_effects=True, vmem_limit_bytes=40 * 1024 * 1024
        ),
    )(out_gate[0], in_gate[0], signal[0], upstream[0], filter_taps, skip_gain[None, :])
    return a[None], b[None], lag


def solution(mesh):
    return jax.shard_map(
        on_device,
        mesh=mesh,
        in_specs=(
            P("dp", "seq", None),
            P("dp", "seq", None),
            P("dp", "seq", None),
            P("dp", "seq", None),
            P("seq", None),
            P(),
        ),
        out_specs=(P("dp", "seq", None), P("dp", "seq", None), P("dp", "seq")),
        check_vma=False,
    )
```

time: 387 us -> 119 us (0.31); the launches traced: 382 us -> 118 us
  waiting for transfers between devices: 203 us -> 0 us
  Pallas kernels: 0 us -> 110 us
  other arithmetic: 50.9 us -> 0 us
  starting transfers between devices: 44.8 us -> 0 us
  matrix products: 32.7 us -> 0 us
  local copies, waits for them, and re-layouts: 36.5 us -> 8.1 us
  between operations: 14.3 us -> 0.65 us
    reduce_scatter x1 -> x0, waiting for transfers between devices: 144 us -> none  [on_device(): lax.psum_scatter(lag_terms, 'dp', scatter_dimension=0, tiled=True)]
    pallas_call x0 -> x1, Pallas kernels: none -> 110 us  [on_device(): pl.pallas_call(kernel, out_shape=(jax.ShapeDtypeStruct((128, 2048), bf16)...]
    all_to_all x4 -> x0, waiting for transfers between devices: 58.4 us -> none  [the longest x1 26.2 us: on_device(): lax.all_to_all(conv_input, 'seq', split_axis=1, concat_axis=0, tiled=True)]
    all_to_all x4 -> x0, starting transfers between devices: 44.8 us -> none  [the longest x1 18.2 us: on_device(): lax.all_to_all(conv_input, 'seq', split_axis=1, concat_axis=0, tiled=True)]
    dot_general x6 -> x0, matrix products: 32.7 us -> none  [the longest x2 9.79 us: forward_dft(): jnp.einsum('pkrc,prqm->qkmc', jnp.stack([real_two, imag_two], 0), inner_t...]
    add x4 -> x0, other arithmetic: 21.2 us -> none  [the longest x2 12.4 us: forward_dft(): both = product[:, :2 * first] + product[:, 2 * first:]]
    another operation x4 -> x0, other arithmetic: 17.6 us -> none  [the longest x2 16.7 us: forward_dft(): jnp.stack([real_two, imag_two], 0)]
    another operation x3 -> x0, local copies, waits for them, and re-layouts: 15 us -> none  [the longest x2 14.7 us: forward_dft(): jnp.stack([real_two, imag_two], 0)]
  transfers between devices with their start and end apart: 5 -> 0, of which waited for: 4 -> 0; matrix products, arithmetic and copies ran while one was open for 9% -> 0% of each run, Pallas kernels for 0% -> 0%
where the time goes in v1:
time: 119 us; the launch traced here: 118 us
  Pallas kernels  110 us (92%)
  local copies, waits for them, and re-layouts  8.1 us (7%)
    pallas_call x1, Pallas kernels, on_device(): pl.pallas_call(kernel, out_shape=(jax.ShapeDtypeStruct((128, 2048), bf16)...  110 us
    unnamed x15, local copies, waits for them, and re-layouts  8.1 us

profile of v1, /device:TPU:1, one launch (start us, length us, event | category | flops | bytes accessed | tf_op | source)
XLA Modules:
  0.0 118.3 jit_solution(14968151301041318354)
XLA Ops:
  0.6 0.0 copy-start.5
  0.6 0.7 copy-done.5
  1.3 0.0 copy-start
  1.3 1.0 copy-done
  2.4 0.0 copy-start.1
  2.4 1.0 copy-done.1
  3.4 0.0 copy-start.2
  3.4 1.0 copy-done.2
  4.5 0.0 copy-start.3
  4.5 1.0 copy-done.3
  5.5 0.0 copy-start.4
  5.5 1.0 copy-done.4
  6.5 109.6 %shard_map.85 = (bf16[128,2048]{1,0:T(8,128)(2,1)S(1)}, bf16[128,2048]{1,0:T(8,128)(2,1)S(1)}, f32[64,128]{1,0:T(8,128)S(1)}) custom-call(bf16[128,2048]{1,0:T(8,128)(2,1)S(1)} %bitcast.7, bf16[128,2048]{1,0:T(8,128)(2,1)S(1)} %bitcast.8, bf16[128,2048]{1,0:T(8,128)(2,1)S(1)} %bitcast.9, bf16[128,2048]{1,0:T(8,128)(2,1)S(1)} %bitcast.10, ...), custom_call_target="tpu_custom_call" | custom-call | tf_op jit(solution)/shard_map/pallas_call | solution.py:293
  116.1 0.8 copy.12
  116.9 0.8 copy.13
  117.7 0.6 copy.14
Async XLA Ops:
  0.6 0.7 copy-start.5
  1.3 1.0 copy-start
  2.4 1.0 copy-start.1
  3.4 1.0 copy-start.2
  4.5 1.0 copy-start.3
  5.5 1.0 copy-start.4

commit v2 on v1

v2 whole, which is shorter than its diff:
```python
import jax
import jax.numpy as jnp
from jax import lax
from jax.experimental import pallas as pl
from jax.experimental.pallas import tpu as pltpu
from jax.sharding import PartitionSpec as P

MESH = pl.DeviceIdType.MESH
f32 = jnp.float32
bf16 = jnp.bfloat16

GROUPS = [[(dx, dz) for dz in (1, 3, 2, 0) if (dx, dz) != (0, 0)] for dx in range(4)]
SLOT = {off: i for i, off in enumerate(off for group in GROUPS for off in group)}


def kernel(
    og_hbm, ig_hbm, sg_hbm, up_hbm, ft_hbm, skip_hbm,
    oa, ob, of,
    og, ig, sg, up, ft, skip,
    gT, uT, hT, g1, u1, H, G, U, BC, R1, bT, Gf, Uf, Bf, HR, Lp, L, LZ, LS, LQ,
    ins, g1s, g1r, u1s, u1r, hs, hr, g2s, g2r, u2s, u2r, b2s, b2r, b1s, b1r, lzs, lzr, lqs, lqr,
):
    dp = lax.axis_index("dp")
    sq = lax.axis_index("seq")
    x, zh = sq // 4, sq % 4
    zl, q = dp // 8, dp % 8

    def seq_index(dx, dz, sign=1):
        return ((x + sign * dx + 4) % 4) * 4 + (zh + sign * dz + 4) % 4

    def seq_dev(dx, dz):
        return (dp, seq_index(dx, dz))

    def q_index(k):
        return (q + k) % 8

    def q_dev(k):
        return (zl * 8 + q_index(k), sq)

    def zl_index(k):
        return (zl + k) % 4

    def zl_dev(k):
        return (zl_index(k) * 8 + q, sq)

    def remote(src, dst, ssem, rsem, dev):
        return pltpu.make_async_remote_copy(
            src_ref=src, dst_ref=dst, send_sem=ssem, recv_sem=rsem,
            device_id=dev, device_id_type=MESH,
        )

    barrier = pltpu.get_barrier_semaphore()
    for group in GROUPS:
        for off in group:
            pl.semaphore_signal(barrier, inc=1, device_id=seq_dev(*off), device_id_type=MESH)
    for k in range(1, 8):
        pl.semaphore_signal(barrier, inc=1, device_id=q_dev(k), device_id_type=MESH)
    for k in range(1, 4):
        pl.semaphore_signal(barrier, inc=1, device_id=zl_dev(k), device_id_type=MESH)

    loads = [
        pltpu.make_async_copy(src, dst, ins.at[i])
        for i, (src, dst) in enumerate(
            [(up_hbm, up), (og_hbm, og), (ft_hbm, ft), (ig_hbm, ig), (sg_hbm, sg), (skip_hbm, skip)]
        )
    ]
    for c in loads:
        c.start()

    def gated(a_ref, b_ref, cols):
        return (a_ref[:, cols].astype(f32) * b_ref[:, cols].astype(f32)).astype(bf16)

    def prepare(a_ref, b_ref, out):
        def body(k, carry):
            cols = pl.ds(pl.multiple_of(k * 128, 128), 128)
            out[k] = gated(a_ref, b_ref, cols).astype(f32).T.astype(bf16)
            return carry
        lax.fori_loop(0, 16, body, 0)

    loads[0].wait()
    loads[1].wait()
    prepare(up, og, gT)

    pl.semaphore_wait(barrier, 25)

    def scatter(n, send, recv, ss, rs):
        copies = []
        for off in GROUPS[n]:
            i = SLOT[off]
            c = remote(send.at[seq_index(*off)], recv.at[x, zh], ss.at[i], rs.at[i], seq_dev(*off))
            c.start()
            copies.append(c)
        return copies

    def sent(copies):
        for c in copies:
            c.wait_send()

    def arrived(copies):
        for c in copies:
            c.wait_recv()

    mine = pl.ds(pl.multiple_of(q * 16, 16), 16)

    def spread(n, first, out, ss, rs):
        copies = []
        xs = (x - n + 4) % 4
        for k in range(1, 8):
            t = pl.ds(pl.multiple_of(q_index(k) * 16, 16), 16)
            c = remote(
                first.at[xs, :, t, :], out.at[xs, :, q],
                ss.at[n, k - 1], rs.at[n, k - 1], q_dev(k),
            )
            c.start()
            copies.append(c)
        out[xs, :, q] = first[xs, :, mine, :]
        return copies

    cg = [scatter(n, gT, g1, g1s, g1r) for n in range(3)]

    loads[2].wait()

    def hbody(k, carry):
        cols = pl.ds(pl.multiple_of(k * 128, 128), 128)
        hT[k] = ft[:, cols].astype(f32).T.astype(bf16)
        return carry
    lax.fori_loop(0, 16, hbody, 0)
    H[sq] = hT[sq, mine, :]
    g1[x, zh] = gT[sq]

    sent(cg[0])
    cg.append(scatter(3, gT, g1, g1s, g1r))
    loads[3].wait()
    loads[4].wait()
    prepare(ig, sg, uT)
    u1[x, zh] = uT[sq]

    cg2 = []
    arrived(cg[0])
    cg2.append(spread(0, g1, G, g2s, g2r))
    sent(cg[1])
    ch = []
    for group in GROUPS:
        for off in group:
            i = SLOT[off]
            c = remote(
                hT.at[seq_index(*off), mine], H.at[sq], hs.at[i], hr.at[i], seq_dev(*off)
            )
            c.start()
            ch.append(c)
    cu = [scatter(0, uT, u1, u1s, u1r)]
    arrived(cg[1])
    cg2.append(spread(1, g1, G, g2s, g2r))
    sent(cg[2])
    cu.append(scatter(1, uT, u1, u1s, u1r))
    arrived(cg[2])
    cg2.append(spread(2, g1, G, g2s, g2r))
    sent(cg[3])
    cu.append(scatter(2, uT, u1, u1s, u1r))
    arrived(cg[3])
    cg2.append(spread(3, g1, G, g2s, g2r))

    row = lax.broadcasted_iota(jnp.int32, (128, 128), 0)
    col = lax.broadcasted_iota(jnp.int32, (128, 128), 1)
    lower = col <= row
    flip = jnp.where(row + col == 127, 1.0, 0.0).astype(bf16)

    arrived(ch)
    HR[...] = jnp.dot(H[...].reshape(256, 128), flip, preferred_element_type=f32)
    sent(cu[0])
    cu.append(scatter(3, uT, u1, u1s, u1r))

    for group in cg2:
        arrived(group)
    Gf[...] = G[...].reshape(2048, 128).astype(f32)

    def shifted(c):
        rows = Gf[pl.ds(c, 128, stride=16), :]
        zero = jnp.zeros((128, 128), f32)
        even = jnp.concatenate([rows, zero], 0).astype(bf16)
        odd = jnp.concatenate([rows[8:], zero, zero[:8]], 0).astype(bf16)
        return [(even, odd)[d % 2][(d // 2) * 16:(d // 2) * 16 + 128] for d in range(16)]

    def conv_body(c, carry):
        gs = shifted(c)
        h = HR[pl.ds(c, 16, stride=16), :]
        prev = jnp.zeros((128, 128), f32)
        total = jnp.zeros((128, 128), f32)
        for e in range(8):
            ws = []
            for d in (2 * e, 2 * e + 1):
                rolled = pltpu.roll(
                    jnp.broadcast_to(h[d:d + 1], (128, 128)), 1, 1, stride=1, stride_axis=0
                )
                ws.append(jnp.where(lower, rolled, prev).astype(bf16))
                prev = rolled
            total += jnp.dot(
                jnp.concatenate([gs[2 * e], gs[2 * e + 1]], 1), jnp.concatenate(ws, 0),
                preferred_element_type=f32,
            )
        Bf[pl.ds(c, 128, stride=16), :] = total
        return carry
    lax.fori_loop(0, 16, conv_body, 0)
    BC[...] = Bf[...].astype(bf16).reshape(4, 4, 8, 16, 128)

    cb2 = []
    for n in range(4):
        xt = (x + n) % 4
        group = []
        for k in range(1, 8):
            c = remote(
                BC.at[xt, :, q_index(k)], R1.at[xt, :, mine, :],
                b2s.at[n, k - 1], b2r.at[n, k - 1], q_dev(k),
            )
            c.start()
            group.append(c)
        R1[xt, :, mine, :] = BC[xt, :, q]
        cb2.append(group)

    def send_back(n):
        arrived(cb2[n])
        copies = []
        for dx, dz in GROUPS[n]:
            i = SLOT[(dx, dz)]
            c = remote(
                R1.at[(x + dx) % 4, (zh + dz) % 4], bT.at[sq],
                b1s.at[i], b1r.at[i], seq_dev(dx, dz),
            )
            c.start()
            copies.append(c)
        return copies

    cu2 = []
    arrived(cu[0])
    cu2.append(spread(0, u1, U, u2s, u2r))
    cb1 = [send_back(0)]
    bT[sq] = R1[x, zh]
    arrived(cu[1])
    cu2.append(spread(1, u1, U, u2s, u2r))
    cb1.append(send_back(1))
    arrived(cu[2])
    cu2.append(spread(2, u1, U, u2s, u2r))
    cb1.append(send_back(2))
    cb1.append(send_back(3))
    arrived(cu[3])
    cu2.append(spread(3, u1, U, u2s, u2r))

    for group in cu2:
        arrived(group)
    Uf[...] = jnp.dot(U[...].reshape(2048, 128), flip, preferred_element_type=f32)

    def lag_body(c, carry):
        gs = shifted(c)
        ut = Uf[pl.ds(c, 128, stride=16), :].T.astype(bf16)
        prev = None
        for e in range(8):
            m = jnp.dot(
                ut, jnp.concatenate([gs[2 * e], gs[2 * e + 1]], 1), preferred_element_type=f32
            )
            for d in (2 * e, 2 * e + 1):
                part = m[:, (d % 2) * 128:(d % 2) * 128 + 128]
                rolled = pltpu.roll(part, 1, 1, stride=1, stride_axis=0)
                if prev is not None:
                    Lp[pl.ds(pl.multiple_of(((d - 1) * 16 + c) * 8, 8), 8), :] = jnp.sum(
                        jnp.where(lower, prev, rolled).reshape(16, 8, 128), 0
                    )
                prev = rolled
        Lp[pl.ds(pl.multiple_of((15 * 16 + c) * 8, 8), 8), :] = jnp.sum(
            jnp.where(lower, prev, 0.0).reshape(16, 8, 128), 0
        )
        return carry
    lax.fori_loop(0, 16, lag_body, 0)

    lags = Lp[pl.ds(0, 256, stride=8), :]
    for k in range(1, 8):
        lags += Lp[pl.ds(k, 256, stride=8), :]
    L[...] = lags.reshape(16, 16, 128)

    def finish(n):
        arrived(cb1[n])

        def body(j, carry):
            blk = ((x - n + 4) % 4) * 4 + j
            cols = pl.ds(pl.multiple_of(blk * 128, 128), 128)
            back = bT[blk].astype(f32).T
            total = back + skip[:, cols] * gated(up, og, cols).astype(f32)
            oa[:, cols] = (total * sg[:, cols].astype(f32)).astype(bf16)
            ob[:, cols] = (total * ig[:, cols].astype(f32)).astype(bf16)
            return carry
        lax.fori_loop(0, 4, body, 0)

    clz = []
    for k in range(1, 4):
        c = remote(
            L.at[pl.ds(zl_index(k) * 4, 4)], LZ.at[k - 1],
            lzs.at[k - 1], lzr.at[k - 1], zl_dev(k),
        )
        c.start()
        clz.append(c)
    loads[5].wait()
    finish(0)
    arrived(clz)
    LS[...] = L[pl.ds(zl * 4, 4)] + LZ[0] + LZ[1] + LZ[2]
    clq = []
    for k in range(1, 8):
        c = remote(
            LS.at[q_index(k) // 2], LQ.at[q], lqs.at[k - 1], lqr.at[k - 1], q_dev(k)
        )
        c.start()
        clq.append(c)
    LQ[q] = LS[q // 2]
    finish(1)
    arrived(clq)
    table = LQ[...].reshape(128, 128).T
    of[...] = jnp.where(q % 2 == 0, table[:64], table[64:]) * (1.0 / 32.0)
    finish(2)
    finish(3)

    for group in [cu[1], cu[2], cu[3], ch, clz, clq] + cg2 + cu2 + cb2 + cb1:
        sent(group)


def on_device(out_gate, in_gate, signal, upstream, filter_taps, skip_gain):
    vm = lambda shape, dtype: pltpu.VMEM(shape, dtype)
    dma = pltpu.SemaphoreType.DMA
    blocks = (16, 128, 128)
    quad = (4, 4, 128, 128)
    owned = (4, 4, 8, 16, 128)
    scratch = [vm((128, 2048), bf16)] * 5 + [vm((1, 2048), f32)] + [
        vm(blocks, bf16), vm(blocks, bf16), vm(blocks, bf16),
        vm(quad, bf16), vm(quad, bf16),
        vm((16, 16, 128), bf16),
        vm(owned, bf16), vm(owned, bf16), vm(owned, bf16),
        vm(quad, bf16), vm(blocks, bf16),
        vm((2048, 128), f32), vm((2048, 128), f32), vm((2048, 128), f32),
        vm((256, 128), f32), vm((2048, 128), f32),
        vm((16, 16, 128), f32), vm((3, 4, 16, 128), f32),
        vm((4, 16, 128), f32), vm((8, 16, 128), f32),
    ]
    scratch.append(dma((6,)))
    for shape in ((15,), (15,), (15,), (4, 7), (4, 7), (4, 7), (15,), (3,), (7,)):
        scratch += [dma(shape), dma(shape)]
    spec = pl.BlockSpec(memory_space=pltpu.VMEM)
    a, b, lag = pl.pallas_call(
        kernel,
        out_shape=(
            jax.ShapeDtypeStruct((128, 2048), bf16),
            jax.ShapeDtypeStruct((128, 2048), bf16),
            jax.ShapeDtypeStruct((64, 128), f32),
        ),
        in_specs=[pl.BlockSpec(memory_space=pltpu.HBM)] * 6,
        out_specs=(spec,) * 3,
        scratch_shapes=scratch,
        compiler_params=pltpu.CompilerParams(
            collective_id=0, has_side_effects=True, vmem_limit_bytes=56 * 1024 * 1024
        ),
    )(out_gate[0], in_gate[0], signal[0], upstream[0], filter_taps, skip_gain[None, :])
    return a[None], b[None], lag


def solution(mesh):
    return jax.shard_map(
        on_device,
        mesh=mesh,
        in_specs=(
            P("dp", "seq", None),
            P("dp", "seq", None),
            P("dp", "seq", None),
            P("dp", "seq", None),
            P("seq", None),
            P(),
        ),
        out_specs=(P("dp", "seq", None), P("dp", "seq", None), P("dp", "seq")),
        check_vma=False,
    )
```

time: 119 us -> 114 us (0.958)
  the two profiles are of different devices: /device:TPU:1 before, /device:TPU:3 now
where the time goes in v2:
time: 114 us
  Pallas kernels  109 us (96%)
  local copies, waits for them, and re-layouts  3.35 us (3%)
    pallas_call x1, Pallas kernels, on_device(): pl.pallas_call(kernel, out_shape=(jax.ShapeDtypeStruct((128, 2048), bf16)...  109 us
    unnamed x7, local copies, waits for them, and re-layouts  3.35 us

profile of v2, /device:TPU:3, one launch (start us, length us, event | category | flops | bytes accessed | tf_op | source)
XLA Modules:
  0.0 113.5 jit_solution(13343654700942060245)
XLA Ops:
  0.6 109.5 %shard_map.85 = (bf16[128,2048]{1,0:T(8,128)(2,1)}, bf16[128,2048]{1,0:T(8,128)(2,1)}, f32[64,128]{1,0:T(8,128)}) custom-call(bf16[128,2048]{1,0:T(8,128)(2,1)} %bitcast.7, bf16[128,2048]{1,0:T(8,128)(2,1)} %bitcast.8, bf16[128,2048]{1,0:T(8,128)(2,1)} %bitcast.9, bf16[128,2048]{1,0:T(8,128)(2,1)} %bitcast.10, bf16[128,2048]{1,0:T(8,128)(2,1)} %ft_hbm.1, ...), custom_call_target="tpu_custom_call" | custom-call | tf_op jit(solution)/shard_map/pallas_call | solution.py:344
  110.1 0.0 copy-start
  110.1 1.9 %copy.12 = bf16[1,128,2048]{2,1,0:T(8,128)(2,1)} copy(bf16[1,128,2048]{2,1,0:T(8,128)(2,1)} %bitcast.12) | data formatting | bytes 1048576
  112.1 0.0 copy-done
  112.1 0.0 copy-start.1
  112.1 0.8 copy.13
  112.9 0.0 copy-done.1
  112.9 0.6 copy.14
Async XLA Ops:
  110.1 2.0 %copy-start = (bf16[128,2048]{1,0:T(8,128)(2,1)S(1)}, bf16[128,2048]{1,0:T(8,128)(2,1)}, u32[]{:S(2)}) copy-start(bf16[128,2048]{1,0:T(8,128)(2,1)} %get-tuple-element.7) | copy-start | bytes 1572868
  112.1 0.8 copy-start.1

commit v3 on v2

--- a/solution.py
+++ b/solution.py
@@ -126,6 +126,28 @@
         return carry
     lax.fori_loop(0, 16, hbody, 0)
     H[sq] = hT[sq, mine, :]
+
+    def start_taps(i, src, dst, dev):
+        c = remote(src, dst, hs.at[i], hr.at[i], dev)
+        c.start()
+        return c
+
+    ch = []
+    cz = []
+    for d in range(1, 4):
+        cz.append(
+            start_taps(d + 2, hT.at[seq_index(zl, d), mine], H.at[sq], seq_dev(zl, d))
+        )
+    for d in range(1, 4):
+        ch.append(start_taps(d - 1, hT.at[seq_index(d, 0), mine], H.at[sq], seq_dev(d, 0)))
+
+    def share_taps():
+        arrived(cz)
+        for d in range(1, 4):
+            tile = H.at[seq_index(zl, d, -1)]
+            for k in range(1, 4):
+                ch.append(start_taps(k * 3 + d + 2, tile, tile, zl_dev(k)))
+
     g1[x, zh] = gT[sq]
 
     sent(cg[0])
@@ -139,18 +161,10 @@
     arrived(cg[0])
     cg2.append(spread(0, g1, G, g2s, g2r))
     sent(cg[1])
-    ch = []
-    for group in GROUPS:
-        for off in group:
-            i = SLOT[off]
-            c = remote(
-                hT.at[seq_index(*off), mine], H.at[sq], hs.at[i], hr.at[i], seq_dev(*off)
-            )
-            c.start()
-            ch.append(c)
     cu = [scatter(0, uT, u1, u1s, u1r)]
     arrived(cg[1])
     cg2.append(spread(1, g1, G, g2s, g2r))
+    share_taps()
     sent(cg[2])
     cu.append(scatter(1, uT, u1, u1s, u1r))
     arrived(cg[2])
@@ -316,7 +330,7 @@
     finish(2)
     finish(3)
 
-    for group in [cu[1], cu[2], cu[3], ch, clz, clq] + cg2 + cu2 + cb2 + cb1:
+    for group in [cu[1], cu[2], cu[3], ch, cz, clz, clq] + cg2 + cu2 + cb2 + cb1:
         sent(group)
 
 
@@ -352,7 +366,7 @@
         out_specs=(spec,) * 3,
         scratch_shapes=scratch,
         compiler_params=pltpu.CompilerParams(
-            collective_id=0, has_side_effects=True, vmem_limit_bytes=56 * 1024 * 1024
+            collective_id=0, has_side_effects=True, vmem_limit_bytes=40 * 1024 * 1024
         ),
     )(out_gate[0], in_gate[0], signal[0], upstream[0], filter_taps, skip_gain[None, :])
     return a[None], b[None], lag

time: 114 us -> 115 us (level)
  the two profiles are of different devices: /device:TPU:3 before, /device:TPU:1 now
where the time goes in v3:
time: 115 us; the launch traced here: 114 us
  Pallas kernels  106 us (92%)
  local copies, waits for them, and re-layouts  8.1 us (7%)
    pallas_call x1, Pallas kernels, on_device(): pl.pallas_call(kernel, out_shape=(jax.ShapeDtypeStruct((128, 2048), bf16)...  106 us
    unnamed x15, local copies, waits for them, and re-layouts  8.1 us

profile of v3, /device:TPU:1, one launch (start us, length us, event | category | flops | bytes accessed | tf_op | source)
XLA Modules:
  0.0 114.4 jit_solution(17826929584080221366)
XLA Ops:
  0.6 0.0 copy-start.5
  0.6 0.7 copy-done.5
  1.3 0.0 copy-start
  1.3 1.0 copy-done
  2.4 0.0 copy-start.1
  2.4 1.0 copy-done.1
  3.4 0.0 copy-start.2
  3.4 1.0 copy-done.2
  4.5 0.0 copy-start.3
  4.5 1.0 copy-done.3
  5.5 0.0 copy-start.4
  5.5 1.0 copy-done.4
  6.5 105.7 %shard_map.85 = (bf16[128,2048]{1,0:T(8,128)(2,1)S(1)}, bf16[128,2048]{1,0:T(8,128)(2,1)S(1)}, f32[64,128]{1,0:T(8,128)S(1)}) custom-call(bf16[128,2048]{1,0:T(8,128)(2,1)S(1)} %bitcast.7, bf16[128,2048]{1,0:T(8,128)(2,1)S(1)} %bitcast.8, bf16[128,2048]{1,0:T(8,128)(2,1)S(1)} %bitcast.9, bf16[128,2048]{1,0:T(8,128)(2,1)S(1)} %bitcast.10, ...), custom_call_target="tpu_custom_call" | custom-call | tf_op jit(solution)/shard_map/pallas_call | solution.py:358
  112.2 0.8 copy.12
  113.0 0.8 copy.13
  113.8 0.6 copy.14
Async XLA Ops:
  0.6 0.7 copy-start.5
  1.3 1.0 copy-start
  2.4 1.0 copy-start.1
  3.4 1.0 copy-start.2
  4.5 1.0 copy-start.3
  5.5 1.0 copy-start.4

commit v4 on v3

--- a/solution.py
+++ b/solution.py
@@ -160,16 +160,16 @@
     cg2 = []
     arrived(cg[0])
     cg2.append(spread(0, g1, G, g2s, g2r))
-    sent(cg[1])
-    cu = [scatter(0, uT, u1, u1s, u1r)]
     arrived(cg[1])
     cg2.append(spread(1, g1, G, g2s, g2r))
     share_taps()
+    sent(cg[1])
     sent(cg[2])
-    cu.append(scatter(1, uT, u1, u1s, u1r))
+    cu = [scatter(0, uT, u1, u1s, u1r)]
     arrived(cg[2])
     cg2.append(spread(2, g1, G, g2s, g2r))
     sent(cg[3])
+    cu.append(scatter(1, uT, u1, u1s, u1r))
     cu.append(scatter(2, uT, u1, u1s, u1r))
     arrived(cg[3])
     cg2.append(spread(3, g1, G, g2s, g2r))
@@ -218,7 +218,8 @@
     BC[...] = Bf[...].astype(bf16).reshape(4, 4, 8, 16, 128)
 
     cb2 = []
-    for n in range(4):
+
+    def turn(n):
         xt = (x + n) % 4
         group = []
         for k in range(1, 8):
@@ -245,16 +246,20 @@
         return copies
 
     cu2 = []
+    turn(0)
+    turn(1)
+    cb1 = [send_back(0)]
+    bT[sq] = R1[x, zh]
+    turn(2)
+    cb1.append(send_back(1))
+    turn(3)
     arrived(cu[0])
     cu2.append(spread(0, u1, U, u2s, u2r))
-    cb1 = [send_back(0)]
-    bT[sq] = R1[x, zh]
     arrived(cu[1])
     cu2.append(spread(1, u1, U, u2s, u2r))
-    cb1.append(send_back(1))
+    cb1.append(send_back(2))
     arrived(cu[2])
     cu2.append(spread(2, u1, U, u2s, u2r))
-    cb1.append(send_back(2))
     cb1.append(send_back(3))
     arrived(cu[3])
     cu2.append(spread(3, u1, U, u2s, u2r))
@@ -366,7 +371,7 @@
         out_specs=(spec,) * 3,
         scratch_shapes=scratch,
         compiler_params=pltpu.CompilerParams(
-            collective_id=0, has_side_effects=True, vmem_limit_bytes=40 * 1024 * 1024
+            collective_id=0, has_side_effects=True, vmem_limit_bytes=56 * 1024 * 1024
         ),
     )(out_gate[0], in_gate[0], signal[0], upstream[0], filter_taps, skip_gain[None, :])
     return a[None], b[None], lag

time: 115 us -> 110 us (0.957)
  local copies, waits for them, and re-layouts: 8.1 us -> 3.35 us
    unnamed x15 -> x7, local copies, waits for them, and re-layouts: 8.1 us -> 3.35 us
where the time goes in v4:
time: 110 us; the launch traced here: 109 us
  Pallas kernels  105 us (95%)
  local copies, waits for them, and re-layouts  3.35 us (3%)
    pallas_call x1, Pallas kernels, on_device(): pl.pallas_call(kernel, out_shape=(jax.ShapeDtypeStruct((128, 2048), bf16)...  105 us
    unnamed x7, local copies, waits for them, and re-layouts  3.35 us

profile of v4, /device:TPU:1, one launch (start us, length us, event | category | flops | bytes accessed | tf_op | source)
XLA Modules:
  0.0 108.8 jit_solution(258333880423687854)
XLA Ops:
  0.6 104.8 %shard_map.85 = (bf16[128,2048]{1,0:T(8,128)(2,1)}, bf16[128,2048]{1,0:T(8,128)(2,1)}, f32[64,128]{1,0:T(8,128)}) custom-call(bf16[128,2048]{1,0:T(8,128)(2,1)} %bitcast.7, bf16[128,2048]{1,0:T(8,128)(2,1)} %bitcast.8, bf16[128,2048]{1,0:T(8,128)(2,1)} %bitcast.9, bf16[128,2048]{1,0:T(8,128)(2,1)} %bitcast.10, bf16[128,2048]{1,0:T(8,128)(2,1)} %ft_hbm.1, ...), custom_call_target="tpu_custom_call" | custom-call | tf_op jit(solution)/shard_map/pallas_call | solution.py:363
  105.4 0.0 copy-start
  105.4 1.9 %copy.12 = bf16[1,128,2048]{2,1,0:T(8,128)(2,1)} copy(bf16[1,128,2048]{2,1,0:T(8,128)(2,1)} %bitcast.12) | data formatting | bytes 1048576
  107.3 0.0 copy-done
  107.4 0.0 copy-start.1
  107.4 0.8 copy.13
  108.1 0.0 copy-done.1
  108.1 0.6 copy.14
Async XLA Ops:
  105.4 2.0 %copy-start = (bf16[128,2048]{1,0:T(8,128)(2,1)S(1)}, bf16[128,2048]{1,0:T(8,128)(2,1)}, u32[]{:S(2)}) copy-start(bf16[128,2048]{1,0:T(8,128)(2,1)} %get-tuple-element.7) | copy-start | bytes 1572868
  107.4 0.8 copy-start.1

commit v5 on v4

--- a/solution.py
+++ b/solution.py
@@ -9,7 +9,7 @@
 f32 = jnp.float32
 bf16 = jnp.bfloat16
 
-GROUPS = [[(dx, dz) for dz in (1, 3, 2, 0) if (dx, dz) != (0, 0)] for dx in range(4)]
+GROUPS = [[(dx, dz) for dz in (2, 1, 3, 0) if (dx, dz) != (0, 0)] for dx in range(4)]
 SLOT = {off: i for i, off in enumerate(off for group in GROUPS for off in group)}
 
 

time: 110 us -> 108 us (0.982)
  Pallas kernels: 105 us -> 102 us
    pallas_call x1, Pallas kernels: 105 us -> 102 us  [on_device(): pl.pallas_call(kernel, out_shape=(jax.ShapeDtypeStruct((128, 2048), bf16)...]
where the time goes in v5:
time: 108 us; the launch traced here: 106 us
  Pallas kernels  102 us (94%)
  local copies, waits for them, and re-layouts  3.35 us (3%)
    pallas_call x1, Pallas kernels, on_device(): pl.pallas_call(kernel, out_shape=(jax.ShapeDtypeStruct((128, 2048), bf16)...  102 us
    unnamed x7, local copies, waits for them, and re-layouts  3.35 us

profile of v5, /device:TPU:1, one launch (start us, length us, event | category | flops | bytes accessed | tf_op | source)
XLA Modules:
  0.0 106.3 jit_solution(15208269165552453660)
XLA Ops:
  0.6 102.3 %shard_map.85 = (bf16[128,2048]{1,0:T(8,128)(2,1)}, bf16[128,2048]{1,0:T(8,128)(2,1)}, f32[64,128]{1,0:T(8,128)}) custom-call(bf16[128,2048]{1,0:T(8,128)(2,1)} %bitcast.7, bf16[128,2048]{1,0:T(8,128)(2,1)} %bitcast.8, bf16[128,2048]{1,0:T(8,128)(2,1)} %bitcast.9, bf16[128,2048]{1,0:T(8,128)(2,1)} %bitcast.10, bf16[128,2048]{1,0:T(8,128)(2,1)} %ft_hbm.1, ...), custom_call_target="tpu_custom_call" | custom-call | tf_op jit(solution)/shard_map/pallas_call | solution.py:363
  102.9 0.0 copy-start
  102.9 1.9 %copy.12 = bf16[1,128,2048]{2,1,0:T(8,128)(2,1)} copy(bf16[1,128,2048]{2,1,0:T(8,128)(2,1)} %bitcast.12) | data formatting | bytes 1048576
  104.8 0.0 copy-done
  104.8 0.0 copy-start.1
  104.8 0.8 copy.13
  105.6 0.0 copy-done.1
  105.6 0.6 copy.14
Async XLA Ops:
  102.9 2.0 %copy-start = (bf16[128,2048]{1,0:T(8,128)(2,1)S(1)}, bf16[128,2048]{1,0:T(8,128)(2,1)}, u32[]{:S(2)}) copy-start(bf16[128,2048]{1,0:T(8,128)(2,1)} %get-tuple-element.7) | copy-start | bytes 1572868
  104.8 0.8 copy-start.1

commit v6 on v5

--- a/solution.py
+++ b/solution.py
@@ -253,16 +253,11 @@
     turn(2)
     cb1.append(send_back(1))
     turn(3)
-    arrived(cu[0])
-    cu2.append(spread(0, u1, U, u2s, u2r))
-    arrived(cu[1])
-    cu2.append(spread(1, u1, U, u2s, u2r))
     cb1.append(send_back(2))
-    arrived(cu[2])
-    cu2.append(spread(2, u1, U, u2s, u2r))
     cb1.append(send_back(3))
-    arrived(cu[3])
-    cu2.append(spread(3, u1, U, u2s, u2r))
+    for n in range(4):
+        arrived(cu[n])
+        cu2.append(spread(n, u1, U, u2s, u2r))
 
     for group in cu2:
         arrived(group)

time: 108 us -> 108 us (level)
  no operation moved by 1% of the time
where the time goes in v6:
time: 108 us; the launch traced here: 107 us
  Pallas kernels  103 us (95%)
  local copies, waits for them, and re-layouts  3.35 us (3%)
    pallas_call x1, Pallas kernels, on_device(): pl.pallas_call(kernel, out_shape=(jax.ShapeDtypeStruct((128, 2048), bf16)...  103 us
    unnamed x7, local copies, waits for them, and re-layouts  3.35 us

profile of v6, /device:TPU:1, one launch (start us, length us, event | category | flops | bytes accessed | tf_op | source)
XLA Modules:
  0.0 107.2 jit_solution(15669228756709667156)
XLA Ops:
  0.6 103.2 %shard_map.85 = (bf16[128,2048]{1,0:T(8,128)(2,1)}, bf16[128,2048]{1,0:T(8,128)(2,1)}, f32[64,128]{1,0:T(8,128)}) custom-call(bf16[128,2048]{1,0:T(8,128)(2,1)} %bitcast.7, bf16[128,2048]{1,0:T(8,128)(2,1)} %bitcast.8, bf16[128,2048]{1,0:T(8,128)(2,1)} %bitcast.9, bf16[128,2048]{1,0:T(8,128)(2,1)} %bitcast.10, bf16[128,2048]{1,0:T(8,128)(2,1)} %ft_hbm.1, ...), custom_call_target="tpu_custom_call" | custom-call | tf_op jit(solution)/shard_map/pallas_call | solution.py:358
  103.9 0.0 copy-start
  103.9 1.9 %copy.12 = bf16[1,128,2048]{2,1,0:T(8,128)(2,1)} copy(bf16[1,128,2048]{2,1,0:T(8,128)(2,1)} %bitcast.12) | data formatting | bytes 1048576
  105.8 0.0 copy-done
  105.8 0.0 copy-start.1
  105.8 0.8 copy.13
  106.6 0.0 copy-done.1
  106.6 0.6 copy.14
Async XLA Ops:
  103.9 2.0 %copy-start = (bf16[128,2048]{1,0:T(8,128)(2,1)S(1)}, bf16[128,2048]{1,0:T(8,128)(2,1)}, u32[]{:S(2)}) copy-start(bf16[128,2048]{1,0:T(8,128)(2,1)} %get-tuple-element.7) | copy-start | bytes 1572868
  105.8 0.8 copy-start.1
